TPU v7x, 32 devices: a whole 2x2x4 slice. The times are simulated.
32 devices in a mesh: frag: 2 (over x), aux: 2 (over core), ao: 8 (over z, y).
Axes of the slice: x: 2, y: 2, z: 4, core: 2. Of those that a mesh axis runs over, the one named last changes fastest.
Arguments:
- factors: bfloat16 [4, 24576, 1024], P(None, ('frag', 'aux'), 'ao'), parts along dimension 1, may hold values from -0.41992188 to 0.41992188
- pairs: int32 [16, 2], P('frag'), parts along dimension 0, may hold values from 0 to 7, as said below
- owners: int32 [16, 2], P('frag'), parts along dimension 0, may hold values from 0 to 7, all different within a row; in each aligned block of 8 rows (0 to 7, 8 to 15, ...) at most 4 rows name the same one
Outputs:
- ktiles: float32 [64, 128, 128], P(('frag', 'ao'), 'aux'), parts along dimension 0
There are 2 independent parts, one for each index of `frag`. A program takes and returns all parts, laid end to end along the dimension named above; each array names one. Nothing has to cross between parts.
Inputs may be any that keep to these rules, and one draw needn't show every extreme that they name: `pairs`: the two blocks of a pair differ; a pair may repeat. The two owners of a pair differ; no ao index owns more than 4 entries, a bound that some block reaches.
All inputs are finite; a program needn't handle non-finite values.
Results may differ from a plain program's by a relative error of at most 0.0003.
Values may be sent and summed in bfloat16 or wider, within the bound.
A program may use at most 128 MiB of HBM per device.

v0:
```python
import jax
import jax.numpy as jnp
from jax import lax
from jax.sharding import PartitionSpec as P

CAP = 4


def slot_table(pairs, owners, n_owner, capacity):
    count = pairs.shape[0]
    owner_flat = jnp.concatenate([owners[:, 0], owners[:, 1]])
    hits = (owner_flat[:, None] == jnp.arange(n_owner, dtype=jnp.int32)[None, :]).astype(jnp.int32)
    ranks = jnp.sum(hits * (jnp.cumsum(hits, axis=0) - 1), axis=1)
    slot_of = owner_flat * capacity + ranks
    match = (slot_of[None, :] == jnp.arange(n_owner * capacity, dtype=jnp.int32)[:, None]).astype(
        jnp.int32
    )
    entry = jnp.sum(match * jnp.arange(2 * count, dtype=jnp.int32)[None, :], axis=1)
    filled = jnp.sum(match, axis=1)
    return (entry, filled)


def on_device(factors, pairs, owners):
    n_ao = lax.axis_size("ao")
    n_aux = lax.axis_size("aux")
    occupied = factors.shape[0]
    block = factors.shape[2]
    half = block // n_aux
    count = pairs.shape[0]
    moved = lax.all_to_all(factors, "ao", split_axis=1, concat_axis=2, tiled=True)
    depth = occupied * moved.shape[1]
    local = moved.reshape(depth, n_ao, block)
    left = jnp.take(local, pairs[:, 0], axis=1)
    right = jnp.take(local, pairs[:, 1], axis=1)
    entry, filled = slot_table(pairs, owners, n_ao, CAP)
    tiles = jnp.einsum("rpa,rpb->pab", left, right, preferred_element_type=jnp.float32)
    upper = tiles.reshape(count, n_aux, half, block).transpose(1, 0, 2, 3)
    mirrored = jnp.einsum("rpa,rpb->pab", right, left, preferred_element_type=jnp.float32)
    lower = mirrored.reshape(count, n_aux, half, block).transpose(1, 0, 2, 3)
    entries = jnp.concatenate([upper, lower], axis=1).reshape(-1, block)
    total_slots = n_ao * CAP
    entry_count = 2 * count
    line_ids = jnp.arange(CAP * half * lax.axis_size(("aux", "ao")), dtype=jnp.int32)
    share = line_ids // (total_slots * half)
    slot = line_ids // half % total_slots
    line = line_ids % half
    source = (share * entry_count + jnp.take(entry, slot)) * half + line
    weight = jnp.take(filled, slot).astype(jnp.float32)
    mine = lax.psum_scatter(
        jnp.take(entries, source, axis=0) * weight[:, None],
        ("aux", "ao"),
        scatter_dimension=0,
        tiled=True,
    )
    return mine.reshape(CAP, half, block)


def solution(mesh):
    in_specs = (P(None, ("frag", "aux"), "ao"), P("frag", None), P("frag", None))
    out_specs = P(("frag", "ao"), "aux", None)
    return jax.shard_map(
        on_device, mesh=mesh, in_specs=in_specs, out_specs=out_specs, check_vma=False
    )
```

profile of v0, /device:TPU:0, one launch (start us, length us, event | category | flops | bytes accessed | tf_op | source)
XLA Modules:
  0.0 279.1 jit_solution(3002821814675780714)
XLA Ops:
  6.5 10.5 %copy.26 = bf16[4,6144,128]{2,0,1:T(4,128)(2,1)} copy(bf16[4,6144,128]{2,1,0:T(8,128)(2,1)} %param.7) | data formatting | bytes 12582912 | tf_op args[0]
  17.0 0.0 copy-start.2
  17.0 0.0 copy-start.1
  17.0 7.4 %all-to-all-start = ((bf16[4,6144,128]{2,0,1:T(4,128)(2,1)}), bf16[4,6144,128]{2,0,1:T(4,128)(2,1)}, u32[]{:S(2)}, u32[]{:S(2)}) async-start(bf16[4,6144,128]{2,0,1:T(4,128)(2,1)} %copy.26), calls=%async_computation | async-start | bytes 12582912 | tf_op jit(solution)/shard_map/all_to_all | solution.py:30
  24.4 0.0 reduce-scatter.2.cloned.1.call-start
  24.5 0.0 copy-done.2
  24.5 0.1 pad_add_fusion
  24.6 0.1 fusion.18
  24.7 0.2 select_reduce_fusion.1
  24.9 0.1 multiply_add_fusion
  24.9 0.1 convert_reduce_fusion
  25.0 0.7 fusion.24
  25.7 0.7 fusion.23
  26.5 19.8 %compare_and_fusion.1 = pred[4096]{0:T(1024)(128)(4,1)S(1)} fusion(s32[]{:T(128)} %bitcast.33, s32[]{:T(128)} %bitcast.32, s32[]{:T(128)} %bitcast.31, s32[]{:T(128)} %bitcast.30, s32[]{:T(128)} %bitcast.29, s32[]{:T(128)} %bitcast.28, s32[]{:T(128)} %bitcast.27, s32[]{:T(128)} %bitcast.26, s32[]{:T(128)} %bitcast.25, s32[]{:T(128)} %bitcast.24, ...), kind=kLoop, calls=%fused_computation.40 | loop fusion | flops 442368 | bytes 4224 | tf_op jit(solution)/shard_map/jit(_take)/and | solution.py:50
  46.3 0.0 copy-done.1
  46.3 19.8 %broadcast_clamp_fusion = s32[4096]{0:T(1024)S(1)} fusion(s32[]{:T(128)} %bitcast.33, s32[]{:T(128)} %bitcast.32, s32[]{:T(128)} %bitcast.31, s32[]{:T(128)} %bitcast.30, s32[]{:T(128)} %bitcast.29, s32[]{:T(128)} %bitcast.28, s32[]{:T(128)} %bitcast.27, s32[]{:T(128)} %bitcast.26, s32[]{:T(128)} %bitcast.25, s32[]{:T(128)} %bitcast.24, s32[]{:T(128)} %bitcast.23, ...), kind=kLoop, calls=%fused_computation.41 | loop fusion | flops 434176 | bytes 16512 | tf_op jit(solution)/shard_map/jit(_take)/gather | solution.py:50
  66.2 0.7 fusion.22
  66.8 0.7 fusion.21
  67.6 19.8 %select_convert_fusion = f32[4096]{0:T(1024)S(1)} fusion(s32[]{:T(128)} %bitcast.77, s32[]{:T(128)} %bitcast.76, s32[]{:T(128)} %bitcast.75, s32[]{:T(128)} %bitcast.74, s32[]{:T(128)} %bitcast.73, s32[]{:T(128)} %bitcast.72, s32[]{:T(128)} %bitcast.71, s32[]{:T(128)} %bitcast.70, s32[]{:T(128)} %bitcast.69, s32[]{:T(128)} %bitcast.68, s32[]{:T(128)} %bitcast.67, ...), kind=kLoop, calls=%fused_computation.38 | loop fusion | flops 364544 | bytes 16512 | tf_op jit(solution)/shard_map/convert_element_type | solution.py:48
  87.4 75.3 %all-to-all-done = bf16[4,6144,128]{2,0,1:T(4,128)(2,1)} async-done(((bf16[4,6144,128]{2,0,1:T(4,128)(2,1)}), bf16[4,6144,128]{2,0,1:T(4,128)(2,1)}, u32[]{:S(2)}, u32[]{:S(2)}) %all-to-all-start) | async-done | bytes 6291488 | tf_op jit(solution)/shard_map/all_to_all | solution.py:30
  162.7 3.6 %copy.27 = bf16[4,6144,128]{2,1,0:T(8,128)(2,1)S(1)} copy(bf16[4,6144,128]{2,0,1:T(4,128)(2,1)} %all-to-all-done) | data formatting | bytes 12582912 | tf_op jit(solution)/shard_map/all_to_all | solution.py:30
  166.3 4.0 %copy.28 = bf16[4,768,8,128]{3,2,1,0:T(8,128)(2,1)S(1)} copy(bf16[4,768,8,128]{3,1,2,0:T(8,128)(2,1)S(1)} %bitcast.97) | data formatting | bytes 12582912 | tf_op jit(solution)/shard_map/all_to_all | solution.py:30
  170.3 3.7 %copy.29 = bf16[3072,8,128]{2,0,1:T(8,128)(2,1)} copy(bf16[3072,8,128]{2,1,0:T(8,128)(2,1)S(1)} %bitcast.98) | data formatting | bytes 12582912 | tf_op jit(solution)/shard_map/reshape | solution.py:32
  174.0 6.8 %gather_fusion.1 = bf16[8,3072,128]{2,1,0:T(8,128)(2,1)} fusion(bf16[3072,8,128]{2,0,1:T(8,128)(2,1)} %copy.29, s32[1024]{0:T(1024)S(1)} %get-tuple-element.82), kind=kCustom, calls=%fused_computation.clone | custom fusion | bytes 12582944 | tf_op jit(solution)/shard_map/jit(_take)/gather | solution.py:33
  180.8 0.0 slice-start
  180.8 6.9 %gather_fusion.2 = bf16[8,3072,128]{2,1,0:T(8,128)(2,1)} fusion(bf16[3072,8,128]{2,0,1:T(8,128)(2,1)} %copy.29, s32[1024]{0:T(1024)S(1)} %get-tuple-element.81), kind=kCustom, calls=%fused_computation.1.clone | custom fusion | bytes 12582944 | tf_op jit(solution)/shard_map/jit(_take)/gather | solution.py:34
  187.6 0.0 slice-start.1
  187.6 0.0 copy-start
  187.6 7.2 %fusion = f32[8,128,128]{2,1,0:T(8,128)S(1)} fusion(bf16[8,3072,128]{2,1,0:T(8,128)(2,1)} %gather_fusion.1, pred[8]{0:T(512)(128)(4,1)S(1)} %get-tuple-element.15, bf16[8,3072,128]{2,1,0:T(8,128)(2,1)} %gather_fusion.2, pred[8]{0:T(512)(128)(4,1)S(1)} %get-tuple-element.9), kind=kOutput, calls=%fused_computation.3 | convolution fusion | flops 811597824 | bytes 13107216 | tf_op jit(solution)/shard_map/rpa,rpb->pab/dot_general | solution.py:38
  194.8 0.0 slice-done
  194.8 0.0 slice-done.1
  194.8 0.5 copy-done
  195.3 2.5 fusion.2
  197.9 0.1 pad_maximum_fusion
  198.0 0.1 copy.33
  198.1 10.8 %gather_fusion = f32[4096,128]{1,0:T(8,128)S(1)} fusion(f32[2048,128]{1,0:T(8,128)S(1)} %bitcast.96, s32[4096]{0:T(1024)S(1)} %broadcast_clamp_fusion), kind=kCustom, calls=%fused_computation.2 | custom fusion | bytes 4210688 | tf_op jit(solution)/shard_map/jit(_take)/gather | solution.py:50
  208.8 2.6 select_multiply_fusion
  211.5 0.0 reduce-scatter.2.cloned.1.call-update
  211.5 60.7 %reduce-scatter.2.cloned.1.call-done = f32[256,128]{1,0:T(8,128)} async-done(((f32[4096,128]{1,0:T(8,128)}), f32[256,128]{1,0:T(8,128)}) %reduce-scatter.2.cloned.1.call-update) | async-done | bytes 131088 | tf_op jit(solution)/shard_map/reduce_scatter | solution.py:49
  (5 shorter events, 0.1 us)
Async XLA Ops:
  17.0 7.5 %copy-start.2 = (s32[8,2]{0,1:T(2,128)S(1)}, s32[8,2]{0,1:T(2,128)}, u32[]{:S(2)}) copy-start(s32[8,2]{0,1:T(2,128)} %param.9) | copy-start | bytes 196
  17.0 29.3 %copy-start.1 = (s32[8,2]{0,1:T(2,128)S(1)}, s32[8,2]{0,1:T(2,128)}, u32[]{:S(2)}) copy-start(s32[8,2]{0,1:T(2,128)} %param.8) | copy-start | bytes 196
  17.0 145.6 %all-to-all-start = ((bf16[4,6144,128]{2,0,1:T(4,128)(2,1)}), bf16[4,6144,128]{2,0,1:T(4,128)(2,1)}, u32[]{:S(2)}, u32[]{:S(2)}) async-start(bf16[4,6144,128]{2,0,1:T(4,128)(2,1)} %copy.26), calls=%async_computation | async-start | bytes 12582912 | tf_op jit(solution)/shard_map/all_to_all | solution.py:30
  24.4 247.8 %reduce-scatter.2.cloned.1.call-start = ((), (), s32[]{:S(2)}) async-start(), calls=%async_computation.2 | async-start | bytes 2228224 | tf_op jit(solution)/shard_map/reduce_scatter | solution.py:49
  180.8 14.1 %slice-start = ((s8[6291456]{0:T(1024)(128)(4,1)}), s8[2097152]{0:T(1024)(128)(4,1)S(1)}, s32[]{:S(2)}) async-start(s8[6291456]{0:T(1024)(128)(4,1)} %bitcast.99), calls=%async_computation.3 | async-start | bytes 4194304
  187.6 7.2 %slice-start.1 = ((s8[6291456]{0:T(1024)(128)(4,1)}), s8[4194304]{0:T(1024)(128)(4,1)S(1)}, s32[]{:S(2)}) async-start(s8[6291456]{0:T(1024)(128)(4,1)} %bitcast.99), calls=%async_computation.4 | async-start | bytes 8388608
  187.6 7.7 %copy-start = (bf16[8,3072,128]{2,1,0:T(8,128)(2,1)S(1)}, bf16[8,3072,128]{2,1,0:T(8,128)(2,1)}, u32[]{:S(2)}) copy-start(bf16[8,3072,128]{2,1,0:T(8,128)(2,1)} %gather_fusion.2) | copy-start | bytes 18874372
Sparse Core Ops, SparseCore 0:
  211.6 60.5 reduce-scatter.1
where the time goes:
time: 280 us; the launch traced here: 279 us
  waiting for transfers between devices  136 us (49%)
  other arithmetic  62.7 us (22%)
  local copies, waits for them, and re-layouts  49.7 us (18%)
  between operations  13.5 us (5%)
  matrix products  9.71 us (3%)
  starting transfers between devices  7.45 us (3%)
    all_to_all x1, waiting for transfers between devices, on_device(): lax.all_to_all(factors, 'ao', split_axis=1, concat_axis=2, tiled=True)  75.3 us
    reduce_scatter x1, waiting for transfers between devices, on_device(): lax.psum_scatter(jnp.take(entries, source, axis=0) * weight[:, None], ('a...  60.7 us
    and x1, other arithmetic, on_device(): jnp.take(entries, source, axis=0) * weight[:, None]  19.8 us
    gather x1, other arithmetic, on_device(): jnp.take(entries, source, axis=0) * weight[:, None]  19.8 us
    convert_element_type x1, other arithmetic, on_device(): weight = jnp.take(filled, slot).astype(jnp.float32)  19.8 us
    unnamed x11, local copies, waits for them, and re-layouts  11 us
    gather x1, local copies, waits for them, and re-layouts, on_device(): jnp.take(entries, source, axis=0) * weight[:, None]  10.8 us
    all_to_all x2, local copies, waits for them, and re-layouts, on_device(): lax.all_to_all(factors, 'ao', split_axis=1, concat_axis=2, tiled=True)  7.65 us
  transfers between devices with their start and end apart: 2, of which 2 were waited for; matrix products, arithmetic and copies ran while one was open for 23% of the time, Pallas kernels for 0%

commit v1 on v0

v1 whole, which is shorter than its diff:
```python
import functools

import jax
import jax.numpy as jnp
from jax import lax
from jax.experimental import pallas as pl
from jax.experimental.pallas import tpu as pltpu
from jax.sharding import PartitionSpec as P

CAP = 4
MESH = pl.DeviceIdType.MESH


def kernel(n_ao, n_aux, occupied, pairs_ref, owners_ref, factors_ref, out_ref, *scratch):
    bufs = scratch[:occupied]
    acc, from_core, from_ao, piece, tiles = scratch[occupied : occupied + 5]
    own_sem, send_sem, recv_sem, core_sem, part_sem, spread_sem, pass_sem = scratch[occupied + 5 :]
    me = lax.axis_index("ao")
    core = lax.axis_index("aux")
    other = 1 - core
    rows, block = bufs[0].shape[1:]
    count = pairs_ref.shape[0]
    half = out_ref.shape[1]
    share = acc.shape[0] // n_aux
    size = share // n_ao
    pieces = block // size

    def peer(k):
        return lax.rem(me + k, n_ao)

    def source(k):
        return lax.rem(me + (n_ao - k), n_ao)

    barrier = pltpu.get_barrier_semaphore()
    for k in range(1, n_ao):
        pl.semaphore_signal(barrier, inc=1, device_id={"ao": peer(k)}, device_id_type=MESH)
    pl.semaphore_signal(barrier, inc=1, device_id={"aux": other}, device_id_type=MESH)
    own = []
    for o in range(occupied):
        copy = pltpu.make_async_copy(
            factors_ref.at[o, pl.ds(pl.multiple_of(me * rows, 16), rows)], bufs[o].at[me], own_sem.at[o]
        )
        copy.start()
        own.append(copy)
    pl.semaphore_wait(barrier, n_ao)

    def move(o, k):
        return pltpu.make_async_remote_copy(
            src_ref=factors_ref.at[o, pl.ds(pl.multiple_of(peer(k) * rows, 16), rows)],
            dst_ref=bufs[o].at[me],
            send_sem=send_sem.at[o, k],
            recv_sem=recv_sem.at[o, k],
            device_id={"ao": peer(k)},
            device_id_type=MESH,
        )

    order = sorted(range(1, n_ao), key=lambda k: -min(k, n_ao - k))
    for o in range(occupied):
        for k in order:
            move(o, k).start()

    entry = [jnp.int32(0)] * CAP
    filled = jnp.int32(0)
    for e in range(2 * count):
        hit = owners_ref[e % count, e // count] == me
        for c in range(CAP):
            entry[c] = jnp.where(jnp.logical_and(hit, filled == c), e, entry[c])
        filled = filled + hit.astype(jnp.int32)

    for o in range(occupied):
        own[o].wait()
        for k in order:
            move(o, k).wait_recv()

        def one_pair(p, carry, o=o):
            left = bufs[o][pairs_ref[p, 0]]
            right = bufs[o][pairs_ref[p, 1]]
            tile = lax.dot_general(
                left, right, (((0,), (0,)), ((), ())), preferred_element_type=jnp.float32
            )
            at = pl.ds(pl.multiple_of(p * block, block), block)
            if o == 0:
                acc[at] = tile
            else:
                acc[at] += tile
            return carry

        lax.fori_loop(0, count, one_pair, 0)

    swap = pltpu.make_async_remote_copy(
        src_ref=acc.at[pl.ds(pl.multiple_of(other * share, share), share)],
        dst_ref=from_core,
        send_sem=core_sem.at[0],
        recv_sem=core_sem.at[1],
        device_id={"aux": other},
        device_id_type=MESH,
    )
    swap.start()
    swap.wait()
    from_core[...] += acc[pl.ds(pl.multiple_of(core * share, share), share)]

    def part(k):
        return pltpu.make_async_remote_copy(
            src_ref=from_core.at[pl.ds(pl.multiple_of(peer(k) * size, size), size)],
            dst_ref=from_ao.at[me],
            send_sem=part_sem.at[0, k],
            recv_sem=part_sem.at[1, k],
            device_id={"ao": peer(k)},
            device_id_type=MESH,
        )

    for k in order:
        part(k).start()
    total = from_core[pl.ds(pl.multiple_of(me * size, size), size)]
    for k in order[::-1]:
        part(k).wait_recv()
        total = total + from_ao[source(k)]
    piece[...] = total

    def place(which_core, index):
        flat = which_core * n_ao + index
        return tiles.at[flat // pieces, lax.rem(flat, pieces)]

    def spread(k):
        return pltpu.make_async_remote_copy(
            src_ref=piece,
            dst_ref=place(core, me),
            send_sem=spread_sem.at[0, k],
            recv_sem=spread_sem.at[1, k],
            device_id={"ao": peer(k)},
            device_id_type=MESH,
        )

    def passed(k):
        return pltpu.make_async_remote_copy(
            src_ref=piece if k == 0 else place(core, source(k)),
            dst_ref=place(core, source(k)),
            send_sem=pass_sem.at[0, k],
            recv_sem=pass_sem.at[1, k],
            device_id={"aux": other},
            device_id_type=MESH,
        )

    for k in order:
        spread(k).start()
    passed(0).start()
    place(core, me)[...] = total
    for k in order[::-1]:
        spread(k).wait_recv()
        passed(k).start()
    for k in range(n_ao):
        passed(k).wait()

    for c in range(CAP):
        e = entry[c]
        mirrored = e >= count
        p = jnp.where(mirrored, e - count, e)
        tile = tiles[p].reshape(block, block)
        flipped = tile.T
        chosen = jnp.where(mirrored, flipped, tile)
        mine = jnp.where(core == 0, chosen[:half], chosen[half:])
        out_ref[c] = jnp.where(filled > c, mine, 0.0)

    for k in order:
        for o in range(occupied):
            move(o, k).wait_send()
        part(k).wait_send()
        spread(k).wait_send()


def on_device(factors, pairs, owners):
    n_ao = lax.axis_size("ao")
    n_aux = lax.axis_size("aux")
    occupied, local, block = factors.shape
    rows = local // n_ao
    count = pairs.shape[0]
    share = count * block // n_aux
    size = share // n_ao
    return pl.pallas_call(
        functools.partial(kernel, n_ao, n_aux, occupied),
        out_shape=jax.ShapeDtypeStruct((CAP, block // n_aux, block), jnp.float32),
        in_specs=[
            pl.BlockSpec(memory_space=pltpu.SMEM),
            pl.BlockSpec(memory_space=pltpu.SMEM),
            pl.BlockSpec(memory_space=pl.ANY),
        ],
        out_specs=pl.BlockSpec(memory_space=pltpu.VMEM),
        scratch_shapes=[pltpu.VMEM((n_ao, rows, block), jnp.bfloat16)] * occupied
        + [
            pltpu.VMEM((count * block, block), jnp.float32),
            pltpu.VMEM((share, block), jnp.float32),
            pltpu.VMEM((n_ao, size, block), jnp.float32),
            pltpu.VMEM((size, block), jnp.float32),
            pltpu.VMEM((count, block // size, size, block), jnp.float32),
            pltpu.SemaphoreType.DMA((occupied,)),
            pltpu.SemaphoreType.DMA((occupied, n_ao)),
            pltpu.SemaphoreType.DMA((occupied, n_ao)),
            pltpu.SemaphoreType.DMA((2,)),
            pltpu.SemaphoreType.DMA((2, n_ao)),
            pltpu.SemaphoreType.DMA((2, n_ao)),
            pltpu.SemaphoreType.DMA((2, n_ao)),
        ],
        compiler_params=pltpu.CompilerParams(
            collective_id=0, has_side_effects=True, vmem_limit_bytes=40 << 20
        ),
        cost_estimate=pl.CostEstimate(
            flops=2 * count * block * block * occupied * rows,
            bytes_accessed=factors.size * 2,
            transcendentals=0,
        ),
    )(pairs, owners, factors)


def solution(mesh):
    in_specs = (P(None, ("frag", "aux"), "ao"), P("frag", None), P("frag", None))
    out_specs = P(("frag", "ao"), "aux", None)
    return jax.shard_map(
        on_device, mesh=mesh, in_specs=in_specs, out_specs=out_specs, check_vma=False
    )
```

time: 280 us -> 167 us (0.60)
  Pallas kernels: 0 us -> 162 us
  waiting for transfers between devices: 136 us -> 0 us
  other arithmetic: 62.7 us -> 0 us
  local copies, waits for them, and re-layouts: 49.7 us -> 4.95 us
  between operations: 13.5 us -> 0.01 us
  matrix products: 9.71 us -> 0 us
  starting transfers between devices: 7.45 us -> 0 us
    pallas_call x0 -> x1, Pallas kernels: none -> 162 us  [on_device(): pl.pallas_call(functools.partial(kernel, n_ao, n_aux, occupied), out_shap...]
    all_to_all x1 -> x0, waiting for transfers between devices: 75.3 us -> none  [on_device(): lax.all_to_all(factors, 'ao', split_axis=1, concat_axis=2, tiled=True)]
    reduce_scatter x1 -> x0, waiting for transfers between devices: 60.7 us -> none  [on_device(): lax.psum_scatter(jnp.take(entries, source, axis=0) * weight[:, None], ('a...]
    gather x7 -> x0, local copies, waits for them, and re-layouts: 27.3 us -> none  [the longest x1 10.8 us: on_device(): jnp.take(entries, source, axis=0) * weight[:, None]]
    convert_element_type x2 -> x0, other arithmetic: 19.9 us -> none  [the longest x1 19.8 us: on_device(): weight = jnp.take(filled, slot).astype(jnp.float32)]
    and x2 -> x0, other arithmetic: 19.8 us -> none  [the longest x1 19.8 us: on_device(): jnp.take(entries, source, axis=0) * weight[:, None]]
    gather x2 -> x0, other arithmetic: 19.8 us -> none  [the longest x1 19.8 us: on_device(): jnp.take(entries, source, axis=0) * weight[:, None]]
    dot_general x2 -> x0, matrix products: 9.71 us -> none  [the longest x1 7.17 us: on_device(): jnp.einsum('rpa,rpb->pab', right, left, preferred_element_type=jnp.float32)]
  transfers between devices with their start and end apart: 2 -> 0, of which waited for: 2 -> 0; matrix products, arithmetic and copies ran while one was open for 23% -> 0% of each run, Pallas kernels for 0% -> 0%
where the time goes in v1:
time: 167 us
  Pallas kernels  162 us (97%)
  local copies, waits for them, and re-layouts  4.95 us (3%)
    pallas_call x1, Pallas kernels, on_device(): pl.pallas_call(functools.partial(kernel, n_ao, n_aux, occupied), out_shap...  162 us
    unnamed x5, local copies, waits for them, and re-layouts  4.95 us

profile of v1, /device:TPU:0, one launch (start us, length us, event | category | flops | bytes accessed | tf_op | source)
XLA Modules:
  0.0 167.1 jit_solution(4029553251180008524)
XLA Ops:
  0.0 0.8 copy.4.pairs_ref
  0.8 0.8 copy.5.owners_ref
  1.5 0.0 copy-start
  1.5 2.8 %copy-done = bf16[4,6144,128]{2,1,0:T(8,128)(2,1)S(1)} copy-done((bf16[4,6144,128]{2,1,0:T(8,128)(2,1)S(1)}, bf16[4,6144,128]{2,1,0:T(8,128)(2,1)}, u32[]{:S(2)}) %copy-start) | copy-done | bytes 6291480
  4.3 162.1 %shard_map.37 = f32[4,64,128]{2,1,0:T(8,128)S(1)} custom-call(s32[8,2]{1,0:T(8,128)S(1)} %copy.4.pairs_ref, s32[8,2]{1,0:T(8,128)S(1)} %copy.5.owners_ref, bf16[4,6144,128]{2,1,0:T(8,128)(2,1)S(1)} %copy-done), custom_call_target="tpu_custom_call" | custom-call | flops 805306368 | bytes 6291456 | tf_op jit(solution)/shard_map/pallas_call | solution.py:179
  166.4 0.7 copy.7
Async XLA Ops:
  1.5 2.8 %copy-start = (bf16[4,6144,128]{2,1,0:T(8,128)(2,1)S(1)}, bf16[4,6144,128]{2,1,0:T(8,128)(2,1)}, u32[]{:S(2)}) copy-start(bf16[4,6144,128]{2,1,0:T(8,128)(2,1)} %factors_ref.1) | copy-start | bytes 18874372

commit v2 on v1

v2 whole, which is shorter than its diff:
```python
import functools

import jax
import jax.numpy as jnp
from jax import lax
from jax.experimental import pallas as pl
from jax.experimental.pallas import tpu as pltpu
from jax.sharding import PartitionSpec as P

CAP = 4
MESH = pl.DeviceIdType.MESH


def chunks(occupied, rows):
    parts = [(o, 0, rows) for o in range(occupied - 1)]
    start = 0
    for size in (rows // 2, rows // 3, rows - rows // 2 - rows // 3):
        parts.append((occupied - 1, start, size))
        start += size
    return parts


def kernel(n_ao, n_aux, parts, pairs_hbm, owners_hbm, factors_ref, out_ref, *scratch):
    bufs = scratch[: len(parts)]
    scratch = scratch[len(parts) :]
    pairs_ref, owners_ref, acc, from_core, far, near, far_total, cross, piece, tiles = scratch[:10]
    table_sem, own_sem, send_sem, recv_sem, core_sem, far_sem, near_sem, cross_sem = scratch[10:18]
    spread_sem, relay_sem, pass_sem = scratch[18:]
    me = lax.axis_index("ao")
    core = lax.axis_index("aux")
    other = 1 - core
    block = out_ref.shape[2]
    rows = factors_ref.shape[1] // n_ao
    count = pairs_ref.shape[1]
    half = out_ref.shape[1]
    share = from_core.shape[0]
    size = share // n_ao
    pieces = block // size
    n_side = n_ao // 2
    first = me // n_side * n_side
    mirror = lax.rem(me + n_side, n_ao)

    def peer(k):
        return lax.rem(me + k, n_ao)

    def near_peer(k):
        return first + lax.rem(me - first + k, n_side)

    def near_source(k):
        return first + lax.rem(me - first + (n_side - k), n_side)

    def mirrored_of(index):
        return lax.rem(index + n_side, n_ao)

    barrier = pltpu.get_barrier_semaphore()
    for k in range(1, n_ao):
        pl.semaphore_signal(barrier, inc=1, device_id={"ao": peer(k)}, device_id_type=MESH)
    pl.semaphore_signal(barrier, inc=1, device_id={"aux": other}, device_id_type=MESH)
    tables = [
        pltpu.make_async_copy(pairs_hbm, pairs_ref, table_sem.at[0]),
        pltpu.make_async_copy(owners_hbm, owners_ref, table_sem.at[1]),
    ]
    own = []
    for i, (o, start, length) in enumerate(parts):
        own.append(
            pltpu.make_async_copy(
                factors_ref.at[o, pl.ds(pl.multiple_of(me * rows + start, 16), length)],
                bufs[i].at[me],
                own_sem.at[i],
            )
        )

    def move(i, k):
        o, start, length = parts[i]
        return pltpu.make_async_remote_copy(
            src_ref=factors_ref.at[o, pl.ds(pl.multiple_of(peer(k) * rows + start, 16), length)],
            dst_ref=bufs[i].at[me],
            send_sem=send_sem.at[i, k],
            recv_sem=recv_sem.at[i, k],
            device_id={"ao": peer(k)},
            device_id_type=MESH,
        )

    order = sorted(range(1, n_ao), key=lambda k: -min(k, n_ao - k))
    pl.semaphore_wait(barrier, n_ao)
    for i in range(len(parts)):
        for k in order:
            move(i, k).start()
    for copy in tables + own:
        copy.start()
    for copy in tables:
        copy.wait()

    entry = [jnp.int32(0)] * CAP
    filled = jnp.int32(0)
    for e in range(2 * count):
        hit = owners_ref[e // count, e % count] == me
        for c in range(CAP):
            entry[c] = jnp.where(jnp.logical_and(hit, filled == c), e, entry[c])
        filled = filled + hit.astype(jnp.int32)

    def tile_part(i, which_core):
        def one_pair(q, carry):
            p = which_core * (count // n_aux) + q
            left = bufs[i][pairs_ref[0, p]]
            right = bufs[i][pairs_ref[1, p]]
            tile = lax.dot_general(
                left, right, (((0,), (0,)), ((), ())), preferred_element_type=jnp.float32
            )
            at = pl.ds(pl.multiple_of(p * block, block), block)
            if i == 0:
                acc[at] = tile
            else:
                acc[at] += tile
            return carry

        lax.fori_loop(0, count // n_aux, one_pair, 0)

    swap = pltpu.make_async_remote_copy(
        src_ref=acc.at[pl.ds(pl.multiple_of(other * share, share), share)],
        dst_ref=from_core,
        send_sem=core_sem.at[0],
        recv_sem=core_sem.at[1],
        device_id={"aux": other},
        device_id_type=MESH,
    )
    for i in range(len(parts)):
        own[i].wait()
        for k in order:
            move(i, k).wait_recv()
        tile_part(i, other)
        if i == len(parts) - 1:
            swap.start()
        tile_part(i, core)
    swap.wait()
    from_core[...] += acc[pl.ds(pl.multiple_of(core * share, share), share)]

    def held(index):
        return from_core.at[pl.ds(pl.multiple_of(index * size, size), size)]

    def collect(k, distant):
        sem = far_sem if distant else near_sem
        return pltpu.make_async_remote_copy(
            src_ref=held(mirrored_of(near_peer(k)) if distant else near_peer(k)),
            dst_ref=(far if distant else near).at[k],
            send_sem=sem.at[0, k],
            recv_sem=sem.at[1, k],
            device_id={"ao": near_peer(k)},
            device_id_type=MESH,
        )

    for k in range(1, n_side):
        collect(k, True).start()
    for k in range(1, n_side):
        collect(k, False).start()
    total = held(mirror)[...]
    for k in range(1, n_side):
        collect(k, True).wait_recv()
        total = total + far[k]
    far_total[...] = total

    def across(src, dst, n):
        return pltpu.make_async_remote_copy(
            src_ref=src,
            dst_ref=dst,
            send_sem=cross_sem.at[0, n],
            recv_sem=cross_sem.at[1, n],
            device_id={"ao": mirror},
            device_id_type=MESH,
        )

    halves = across(far_total, cross, 0)
    halves.start()
    total = held(me)[...]
    for k in range(1, n_side):
        collect(k, False).wait_recv()
        total = total + near[k]
    halves.wait_recv()
    total = total + cross[...]
    piece[...] = total

    def place(which_core, index):
        flat = which_core * n_ao + index
        return tiles.at[flat // pieces, lax.rem(flat, pieces)]

    def spread(k, relayed):
        sem = relay_sem if relayed else spread_sem
        return pltpu.make_async_remote_copy(
            src_ref=place(core, mirror) if relayed else piece,
            dst_ref=place(core, mirror if relayed else me),
            send_sem=sem.at[0, k],
            recv_sem=sem.at[1, k],
            device_id={"ao": near_peer(k)},
            device_id_type=MESH,
        )

    def passed(n, index, src=None):
        return pltpu.make_async_remote_copy(
            src_ref=place(core, index) if src is None else src,
            dst_ref=place(core, index),
            send_sem=pass_sem.at[0, n],
            recv_sem=pass_sem.at[1, n],
            device_id={"aux": other},
            device_id_type=MESH,
        )

    swapped = across(piece, place(core, me), 1)
    swapped.start()
    for k in range(1, n_side):
        spread(k, False).start()
    passes = [passed(0, me, piece)]
    passes[-1].start()
    place(core, me)[...] = total
    swapped.wait_recv()
    for k in range(1, n_side):
        spread(k, True).start()
    passes.append(passed(n_side, mirror))
    passes[-1].start()
    for relayed in (False, True):
        for k in range(1, n_side):
            spread(k, relayed).wait_recv()
            index = near_source(k)
            passes.append(
                passed(k + n_side, mirrored_of(index)) if relayed else passed(k, index)
            )
            passes[-1].start()
    for copy in passes:
        copy.wait()

    for c in range(CAP):
        e = entry[c]
        mirrored = e >= count
        p = jnp.where(mirrored, e - count, e)
        tile = tiles[p].reshape(block, block)
        chosen = jnp.where(mirrored, tile.T, tile)
        mine = jnp.where(core == 0, chosen[:half], chosen[half:])
        out_ref[c] = jnp.where(filled > c, mine, 0.0)

    for i in range(len(parts)):
        for k in order:
            move(i, k).wait_send()
    for k in range(1, n_side):
        for second in (False, True):
            collect(k, second).wait_send()
            spread(k, second).wait_send()
    halves.wait_send()
    swapped.wait_send()


def on_device(factors, pairs, owners):
    n_ao = lax.axis_size("ao")
    n_aux = lax.axis_size("aux")
    occupied, local, block = factors.shape
    rows = local // n_ao
    count = pairs.shape[0]
    share = count * block // n_aux
    size = share // n_ao
    n_side = n_ao // 2
    parts = chunks(occupied, rows)
    dma = pltpu.SemaphoreType.DMA
    f32 = jnp.float32
    return pl.pallas_call(
        functools.partial(kernel, n_ao, n_aux, parts),
        out_shape=jax.ShapeDtypeStruct((CAP, block // n_aux, block), f32),
        in_specs=[pl.BlockSpec(memory_space=pl.ANY)] * 3,
        out_specs=pl.BlockSpec(memory_space=pltpu.VMEM),
        scratch_shapes=[
            pltpu.VMEM((n_ao, length, block), jnp.bfloat16) for _, _, length in parts
        ]
        + [
            pltpu.SMEM((2, count), jnp.int32),
            pltpu.SMEM((2, count), jnp.int32),
            pltpu.VMEM((count * block, block), f32),
            pltpu.VMEM((share, block), f32),
            pltpu.VMEM((n_side, size, block), f32),
            pltpu.VMEM((n_side, size, block), f32),
            pltpu.VMEM((size, block), f32),
            pltpu.VMEM((size, block), f32),
            pltpu.VMEM((size, block), f32),
            pltpu.VMEM((count, block // size, size, block), f32),
            dma((2,)),
            dma((len(parts),)),
            dma((len(parts), n_ao)),
            dma((len(parts), n_ao)),
            dma((2,)),
            dma((2, n_side)),
            dma((2, n_side)),
            dma((2, 2)),
            dma((2, n_side)),
            dma((2, n_side)),
            dma((2, n_ao)),
        ],
        compiler_params=pltpu.CompilerParams(
            collective_id=0, has_side_effects=True, vmem_limit_bytes=58 << 20
        ),
        cost_estimate=pl.CostEstimate(
            flops=2 * count * block * block * occupied * rows,
            bytes_accessed=factors.size * 2,
            transcendentals=0,
        ),
    )(pairs.T, owners.T, factors)


def solution(mesh):
    in_specs = (P(None, ("frag", "aux"), "ao"), P("frag", None), P("frag", None))
    out_specs = P(("frag", "ao"), "aux", None)
    return jax.shard_map(
        on_device, mesh=mesh, in_specs=in_specs, out_specs=out_specs, check_vma=False
    )
```

time: 167 us -> 163 us (0.976)
  local copies, waits for them, and re-layouts: 4.95 us -> 1.57 us
    unnamed x5 -> x1, local copies, waits for them, and re-layouts: 4.95 us -> 1.57 us
where the time goes in v2:
time: 163 us
  Pallas kernels  161 us (99%)
    pallas_call x1, Pallas kernels, on_device(): pl.pallas_call(functools.partial(kernel, n_ao, n_aux, parts), out_shape=j...  161 us

profile of v2, /device:TPU:0, one launch (start us, length us, event | category | flops | bytes accessed | tf_op | source)
XLA Modules:
  0.0 162.9 jit_solution(4078856622615847160)
XLA Ops:
  0.0 161.3 %shard_map.37 = f32[4,64,128]{2,1,0:T(8,128)} custom-call(s32[2,8]{1,0:T(2,128)} %bitcast.2, s32[2,8]{1,0:T(2,128)} %bitcast.3, bf16[4,6144,128]{2,1,0:T(8,128)(2,1)} %factors_ref.1), custom_call_target="tpu_custom_call" | custom-call | flops 805306368 | bytes 6291456 | tf_op jit(solution)/shard_map/pallas_call | solution.py:262
  161.3 1.6 copy.5

commit v3 on v2

--- a/solution.py
+++ b/solution.py
@@ -12,12 +12,10 @@
 
 
 def chunks(occupied, rows):
-    parts = [(o, 0, rows) for o in range(occupied - 1)]
-    start = 0
-    for size in (rows // 2, rows // 3, rows - rows // 2 - rows // 3):
-        parts.append((occupied - 1, start, size))
-        start += size
-    return parts
+    first = max(1, occupied - 1)
+    parts = [(0, first, 0, rows)] + [(o, 1, 0, rows) for o in range(first, occupied - 1)]
+    last = rows // 3
+    return parts + [(occupied - 1, 1, 0, rows - last), (occupied - 1, 1, rows - last, last)]
 
 
 def kernel(n_ao, n_aux, parts, pairs_hbm, owners_hbm, factors_ref, out_ref, *scratch):
@@ -61,19 +59,22 @@
         pltpu.make_async_copy(owners_hbm, owners_ref, table_sem.at[1]),
     ]
     own = []
-    for i, (o, start, length) in enumerate(parts):
+    for i, (o, many, start, length) in enumerate(parts):
         own.append(
             pltpu.make_async_copy(
-                factors_ref.at[o, pl.ds(pl.multiple_of(me * rows + start, 16), length)],
+                factors_ref.at[
+                    pl.ds(o, many), pl.ds(pl.multiple_of(me * rows + start, 16), length)
+                ],
                 bufs[i].at[me],
                 own_sem.at[i],
             )
         )
 
     def move(i, k):
-        o, start, length = parts[i]
-        return pltpu.make_async_remote_copy(
-            src_ref=factors_ref.at[o, pl.ds(pl.multiple_of(peer(k) * rows + start, 16), length)],
+        o, many, start, length = parts[i]
+        at = pl.ds(pl.multiple_of(peer(k) * rows + start, 16), length)
+        return pltpu.make_async_remote_copy(
+            src_ref=factors_ref.at[pl.ds(o, many), at],
             dst_ref=bufs[i].at[me],
             send_sem=send_sem.at[i, k],
             recv_sem=recv_sem.at[i, k],
@@ -102,8 +103,8 @@
     def tile_part(i, which_core):
         def one_pair(q, carry):
             p = which_core * (count // n_aux) + q
-            left = bufs[i][pairs_ref[0, p]]
-            right = bufs[i][pairs_ref[1, p]]
+            left = bufs[i][pairs_ref[0, p]].reshape(-1, block)
+            right = bufs[i][pairs_ref[1, p]].reshape(-1, block)
             tile = lax.dot_general(
                 left, right, (((0,), (0,)), ((), ())), preferred_element_type=jnp.float32
             )
@@ -114,7 +115,7 @@
                 acc[at] += tile
             return carry
 
-        lax.fori_loop(0, count // n_aux, one_pair, 0)
+        lax.fori_loop(0, count // n_aux, one_pair, 0, unroll=4)
 
     swap = pltpu.make_async_remote_copy(
         src_ref=acc.at[pl.ds(pl.multiple_of(other * share, share), share)],
@@ -265,7 +266,7 @@
         in_specs=[pl.BlockSpec(memory_space=pl.ANY)] * 3,
         out_specs=pl.BlockSpec(memory_space=pltpu.VMEM),
         scratch_shapes=[
-            pltpu.VMEM((n_ao, length, block), jnp.bfloat16) for _, _, length in parts
+            pltpu.VMEM((n_ao, many, length, block), jnp.bfloat16) for _, many, _, length in parts
         ]
         + [
             pltpu.SMEM((2, count), jnp.int32),
@@ -291,7 +292,7 @@
             dma((2, n_ao)),
         ],
         compiler_params=pltpu.CompilerParams(
-            collective_id=0, has_side_effects=True, vmem_limit_bytes=58 << 20
+            collective_id=0, has_side_effects=True, vmem_limit_bytes=57 << 20
         ),
         cost_estimate=pl.CostEstimate(
             flops=2 * count * block * block * occupied * rows,

time: 163 us -> 162 us (level)
  no operation moved by 1% of the time
where the time goes in v3:
time: 162 us; the launch traced here: 161 us
  Pallas kernels  160 us (99%)
    pallas_call x1, Pallas kernels, on_device(): pl.pallas_call(functools.partial(kernel, n_ao, n_aux, parts), out_shape=j...  160 us

profile of v3, /device:TPU:0, one launch (start us, length us, event | category | flops | bytes accessed | tf_op | source)
XLA Modules:
  0.0 161.5 jit_solution(12789688874251875298)
XLA Ops:
  0.0 159.9 %shard_map.37 = f32[4,64,128]{2,1,0:T(8,128)} custom-call(s32[2,8]{1,0:T(2,128)} %bitcast.2, s32[2,8]{1,0:T(2,128)} %bitcast.3, bf16[4,6144,128]{2,1,0:T(8,128)(2,1)} %factors_ref.1), custom_call_target="tpu_custom_call" | custom-call | flops 805306368 | bytes 6291456 | tf_op jit(solution)/shard_map/pallas_call | solution.py:263
  159.9 1.6 copy.5

commit v4 on v3

--- a/solution.py
+++ b/solution.py
@@ -262,7 +262,7 @@
     f32 = jnp.float32
     return pl.pallas_call(
         functools.partial(kernel, n_ao, n_aux, parts),
-        out_shape=jax.ShapeDtypeStruct((CAP, block // n_aux, block), f32),
+        out_shape=pltpu.VMEM((CAP, block // n_aux, block), f32),
         in_specs=[pl.BlockSpec(memory_space=pl.ANY)] * 3,
         out_specs=pl.BlockSpec(memory_space=pltpu.VMEM),
         scratch_shapes=[

time: 162 us -> 160 us (0.988)
  no operation moved by 1% of the time
where the time goes in v4:
time: 160 us
  Pallas kernels  159 us (99%)
    pallas_call x1, Pallas kernels, on_device(): pl.pallas_call(functools.partial(kernel, n_ao, n_aux, parts), out_shape=p...  159 us

profile of v4, /device:TPU:0, one launch (start us, length us, event | category | flops | bytes accessed | tf_op | source)
XLA Modules:
  0.0 159.9 jit_solution(17567844546871448447)
XLA Ops:
  0.0 159.2 %shard_map.37 = f32[4,64,128]{2,1,0:T(8,128)S(1)} custom-call(s32[2,8]{1,0:T(2,128)} %bitcast.2, s32[2,8]{1,0:T(2,128)} %bitcast.3, bf16[4,6144,128]{2,1,0:T(8,128)(2,1)} %factors_ref.1), custom_call_target="tpu_custom_call" | custom-call | flops 805306368 | bytes 6291456 | tf_op jit(solution)/shard_map/pallas_call | solution.py:263
  159.2 0.7 copy.5

commit v5 on v4

--- a/solution.py
+++ b/solution.py
@@ -14,7 +14,7 @@
 def chunks(occupied, rows):
     first = max(1, occupied - 1)
     parts = [(0, first, 0, rows)] + [(o, 1, 0, rows) for o in range(first, occupied - 1)]
-    last = rows // 3
+    last = rows // 6
     return parts + [(occupied - 1, 1, 0, rows - last), (occupied - 1, 1, rows - last, last)]
 
 
@@ -134,7 +134,13 @@
             swap.start()
         tile_part(i, core)
     swap.wait()
-    from_core[...] += acc[pl.ds(pl.multiple_of(core * share, share), share)]
+
+    def add_own(index):
+        wide = n_side * size
+        at = pl.ds(pl.multiple_of(index * size, wide), wide)
+        from_core[at] += acc[pl.ds(pl.multiple_of(core * share + index * size, wide), wide)]
+
+    add_own(n_side - first)
 
     def held(index):
         return from_core.at[pl.ds(pl.multiple_of(index * size, size), size)]
@@ -152,6 +158,7 @@
 
     for k in range(1, n_side):
         collect(k, True).start()
+    add_own(first)
     for k in range(1, n_side):
         collect(k, False).start()
     total = held(mirror)[...]

time: 160 us -> 160 us (level)
  no operation moved by 1% of the time
where the time goes in v5:
time: 160 us
  Pallas kernels  160 us (100%)
    pallas_call x1, Pallas kernels, on_device(): pl.pallas_call(functools.partial(kernel, n_ao, n_aux, parts), out_shape=p...  160 us

profile of v5, /device:TPU:0, one launch (start us, length us, event | category | flops | bytes accessed | tf_op | source)
XLA Modules:
  0.0 160.3 jit_solution(9497667475034718493)
XLA Ops:
  0.0 159.6 %shard_map.37 = f32[4,64,128]{2,1,0:T(8,128)S(1)} custom-call(s32[2,8]{1,0:T(2,128)} %bitcast.2, s32[2,8]{1,0:T(2,128)} %bitcast.3, bf16[4,6144,128]{2,1,0:T(8,128)(2,1)} %factors_ref.1), custom_call_target="tpu_custom_call" | custom-call | flops 805306368 | bytes 6291456 | tf_op jit(solution)/shard_map/pallas_call | solution.py:270
  159.6 0.7 copy.5
